TPU v7x, 1024 devices: a whole 8x8x8 slice. The times are simulated.
1024 devices in a mesh: expert: 64 (over z_hi, y, core), dp: 16 (over z_lo, x).
Axes of the slice: x: 8, y: 8, z: 8 (z_hi: 4, z_lo: 2; z = z_hi * 2 + z_lo), core: 2. Of those that a mesh axis runs over, the one named last changes fastest.
Arguments:
- dy_values: bfloat16 [16384, 4096], P('expert', 'dp'), may hold values from -6 to 6
- dy_scales: bfloat16 [16384, 32], P('expert', 'dp'), may hold values from 0.25 to 4
- expert_ids: int32 [16384, 1], P('expert'), may hold values from 0 to 63; in each aligned block of 256 rows (0 to 255, 256 to 511, ...) at most 8 rows name the same one
- saved_pre: bfloat16 [32768, 2048], P('expert'), may hold values from -6 to 6
- w_gate: bfloat16 [64, 4096, 1024], P('expert', 'dp'), may hold values from -0.1875 to 0.1875
- w_up: bfloat16 [64, 4096, 1024], P('expert', 'dp'), may hold values from -0.1875 to 0.1875
- w_down: bfloat16 [64, 4096, 1024], P('expert', 'dp'), may hold values from -0.09375 to 0.09375
Outputs:
- grad_input: bfloat16 [16384, 4096], P('expert', 'dp')
- grad_down: float32 [64, 4096, 1024], P('expert', 'dp')
Inputs may be any that keep to these rules, and one draw needn't show every extreme that they name: `expert_ids`: among the rows of one index of expert (aligned blocks of 256 rows) no expert occurs more than 8 times.
All inputs are finite; a program needn't handle non-finite values.
Results may differ from a plain program's by a relative error of at most 0.0057.
Values may be sent and summed in bfloat16 or wider, within the bound.
A program may use at most 32 MiB of HBM per device.

v0:
```python
import jax
import jax.numpy as jnp
from jax import lax
from jax.sharding import PartitionSpec as P


def dequantize(values, scales):
    row_count, feature_count = values.shape
    block_count = scales.shape[1]
    blocked = values.astype(jnp.float32).reshape(
        row_count, block_count, feature_count // block_count
    )
    blocked = blocked * scales.astype(jnp.float32)[:, :, None]
    return blocked.reshape(row_count, feature_count).astype(jnp.bfloat16)


def swiglu_parts(hidden_grad, gate_pre, up_pre):
    sigmoid_gate = jax.nn.sigmoid(gate_pre)
    d_gate = hidden_grad * up_pre * sigmoid_gate * (1.0 + gate_pre * (1.0 - sigmoid_gate))
    d_up = hidden_grad * jax.nn.silu(gate_pre)
    return (d_gate.astype(jnp.bfloat16), d_up.astype(jnp.bfloat16))


def per_device(dy_values, dy_scales, expert_ids, saved_pre, w_gate, w_up, w_down):
    groups = lax.axis_size("expert")
    slot_count = saved_pre.shape[0]
    per_expert = slot_count // groups
    hidden_width = w_down.shape[2]
    feature_count = dy_values.shape[1]
    route_ids = expert_ids[:, 0]
    onehot = (route_ids[:, None] == jnp.arange(groups, dtype=jnp.int32)[None, :]).astype(jnp.int32)
    earlier = jnp.cumsum(onehot, axis=0) - onehot
    position = route_ids * per_expert + jnp.sum(earlier * onehot, axis=1)
    out_values = jnp.zeros((slot_count, feature_count), jnp.bfloat16).at[position].set(dy_values)
    out_scales = (
        jnp.zeros((slot_count, dy_scales.shape[1]), jnp.bfloat16).at[position].set(dy_scales)
    )
    got_values, got_scales = (
        lax.all_to_all(out_values, "expert", split_axis=0, concat_axis=0, tiled=True),
        lax.all_to_all(out_scales, "expert", split_axis=0, concat_axis=0, tiled=True),
    )
    received = dequantize(got_values, got_scales)
    gate_full = saved_pre[:, :hidden_width].astype(jnp.float32)
    up_full = saved_pre[:, hidden_width:].astype(jnp.float32)
    hidden = (jax.nn.silu(gate_full) * up_full).astype(jnp.bfloat16)
    partial_grad = jnp.dot(received, w_down[0], preferred_element_type=jnp.float32)
    hidden_grad = lax.psum(partial_grad, "dp")
    d_gate, d_up = swiglu_parts(hidden_grad, gate_full, up_full)
    pre_grad = jnp.concatenate([d_gate, d_up], axis=1)
    paired = jnp.concatenate([w_gate[0], w_up[0]], axis=1)
    slot_grad = lax.dot_general(
        pre_grad, paired, (((1,), (1,)), ((), ())), preferred_element_type=jnp.float32
    ).astype(jnp.bfloat16)
    returned = lax.all_to_all(slot_grad, "expert", split_axis=0, concat_axis=0, tiled=True)
    grad_input = returned[position]
    grad_down = lax.dot_general(
        received, hidden, (((0,), (0,)), ((), ())), preferred_element_type=jnp.float32
    )
    return (grad_input, grad_down[None])


def solution(mesh):
    return jax.shard_map(
        per_device,
        mesh=mesh,
        in_specs=(
            P("expert", "dp"),
            P("expert", "dp"),
            P("expert", None),
            P("expert", None),
            P("expert", "dp", None),
            P("expert", "dp", None),
            P("expert", "dp", None),
        ),
        out_specs=(P("expert", "dp"), P("expert", "dp", None)),
        check_vma=False,
    )
```

profile of v0, /device:TPU:1, one launch (start us, length us, event | category | flops | bytes accessed | tf_op | source)
XLA Modules:
  0.0 258.8 jit_solution(15943962658716976931)
XLA Ops:
  7.2 0.0 copy-start
  7.2 0.7 fusion.37
  7.9 0.6 reduce-window.6
  8.5 0.2 slice_reduce_fusion
  8.8 0.8 fusion.34
  9.5 0.7 compare_select_fusion
  10.2 0.8 copy.20
  11.1 1.2 scatter_custom_fusion.1
  12.3 1.1 copy.21
  13.3 23.5 %all-to-all-start.1 = ((bf16[64,8,2]{1,2,0:T(2,128)(2,1)}), bf16[64,8,2]{1,2,0:T(2,128)(2,1)S(1)}, u32[]{:S(2)}, u32[]{:S(2)}) async-start(bf16[64,8,2]{1,2,0:T(2,128)(2,1)} %copy.21), calls=%async_computation.1 | async-start | bytes 65536 | tf_op jit(solution)/shard_map/all_to_all | solution.py:40
  36.9 2.5 scatter_custom_fusion
  39.4 9.1 %all-to-all-done.1 = bf16[64,8,2]{1,2,0:T(2,128)(2,1)S(1)} async-done(((bf16[64,8,2]{1,2,0:T(2,128)(2,1)}), bf16[64,8,2]{1,2,0:T(2,128)(2,1)S(1)}, u32[]{:S(2)}, u32[]{:S(2)}) %all-to-all-start.1) | async-done | bytes 2080 | tf_op jit(solution)/shard_map/all_to_all | solution.py:40
  48.5 4.7 %all-to-all-start = ((bf16[64,8,256]{2,1,0:T(8,128)(2,1)}), bf16[64,8,256]{2,1,0:T(8,128)(2,1)S(1)}, u32[]{:S(2)}, u32[]{:S(2)}) async-start(bf16[64,8,256]{2,1,0:T(8,128)(2,1)} %bitcast.5), calls=%async_computation | async-start | bytes 524288 | tf_op jit(solution)/shard_map/all_to_all | solution.py:39
  53.2 0.0 all-reduce.2.cloned.1.call-start
  53.3 0.1 copy.22
  53.4 0.2 copy.25
  53.5 13.7 %all-to-all-done = bf16[64,8,256]{2,1,0:T(8,128)(2,1)S(1)} async-done(((bf16[64,8,256]{2,1,0:T(8,128)(2,1)}), bf16[64,8,256]{2,1,0:T(8,128)(2,1)S(1)}, u32[]{:S(2)}, u32[]{:S(2)}) %all-to-all-start) | async-done | bytes 262176 | tf_op jit(solution)/shard_map/all_to_all | solution.py:39
  67.2 0.3 reshape.58
  67.5 0.7 multiply_convert_fusion.1
  68.2 0.0 copy-done
  68.2 0.0 copy-start.1
  68.2 1.7 fusion.24
  69.9 0.0 all-reduce.2.cloned.1.call-update
  70.0 138.6 %all-reduce.2.cloned.1.call-done = f32[512,1024]{1,0:T(8,128)} async-done(((f32[512,1024]{1,0:T(8,128)}), f32[512,1024]{1,0:T(8,128)}) %all-reduce.2.cloned.1.call-update) | async-done | bytes 2097168 | tf_op jit(solution)/shard_map/psum | solution.py:47
  208.5 0.0 copy-done.1
  208.5 0.0 copy-start.2
  208.5 0.0 copy-start.3
  208.5 2.7 %fusion.2 = (bf16[512,1024]{1,0:T(8,128)(2,1)S(1)}, bf16[512,1024]{1,0:T(8,128)(2,1)S(1)}) fusion(f32[512,1024]{1,0:T(8,128)} %all-reduce.2.cloned.1.call-done, bf16[512,2048]{1,0:T(8,128)(2,1)S(1)} %copy-done.1), kind=kLoop, calls=%fused_computation.10 | loop fusion | flops 7864320 | bytes 6291456 | tf_op jit(solution)/shard_map/convert_element_type | solution.py:21
  211.3 0.0 copy-done.2
  211.3 0.0 copy-done.3
  211.3 1.4 fusion.15
  212.7 23.5 %all-to-all-start.2 = ((bf16[64,8,256]{2,1,0:T(8,128)(2,1)}), bf16[64,8,256]{2,1,0:T(8,128)(2,1)S(1)}, u32[]{:S(2)}, u32[]{:S(2)}) async-start(bf16[64,8,256]{2,1,0:T(8,128)(2,1)} %fusion.15), calls=%async_computation.2 | async-start | bytes 524288 | tf_op jit(solution)/shard_map/all_to_all | solution.py:54
  236.3 0.6 mul.56
  236.9 1.9 convolution_bitcast_fusion
  238.8 11.3 %all-to-all-done.2 = bf16[64,8,256]{2,1,0:T(8,128)(2,1)S(1)} async-done(((bf16[64,8,256]{2,1,0:T(8,128)(2,1)}), bf16[64,8,256]{2,1,0:T(8,128)(2,1)S(1)}, u32[]{:S(2)}, u32[]{:S(2)}) %all-to-all-start.2) | async-done | bytes 262176 | tf_op jit(solution)/shard_map/all_to_all | solution.py:54
  250.1 1.8 gather_fusion
  (3 shorter events, 0.0 us)
Async XLA Ops:
  7.2 61.0 %copy-start = (bf16[1,256,1024]{2,1,0:T(8,128)(2,1)S(1)}, bf16[1,256,1024]{2,1,0:T(8,128)(2,1)}, u32[]{:S(2)}) copy-start(bf16[1,256,1024]{2,1,0:T(8,128)(2,1)} %param.13) | copy-start | bytes 1572868
  13.3 35.2 %all-to-all-start.1 = ((bf16[64,8,2]{1,2,0:T(2,128)(2,1)}), bf16[64,8,2]{1,2,0:T(2,128)(2,1)S(1)}, u32[]{:S(2)}, u32[]{:S(2)}) async-start(bf16[64,8,2]{1,2,0:T(2,128)(2,1)} %copy.21), calls=%async_computation.1 | async-start | bytes 65536 | tf_op jit(solution)/shard_map/all_to_all | solution.py:40
  48.5 18.7 %all-to-all-start = ((bf16[64,8,256]{2,1,0:T(8,128)(2,1)}), bf16[64,8,256]{2,1,0:T(8,128)(2,1)S(1)}, u32[]{:S(2)}, u32[]{:S(2)}) async-start(bf16[64,8,256]{2,1,0:T(8,128)(2,1)} %bitcast.5), calls=%async_computation | async-start | bytes 524288 | tf_op jit(solution)/shard_map/all_to_all | solution.py:39
  53.2 155.3 %all-reduce.2.cloned.1.call-start = ((), (), s32[]{:S(2)}) async-start(), calls=%async_computation.3 | async-start | bytes 4194304 | tf_op jit(solution)/shard_map/psum | solution.py:47
  68.2 140.4 %copy-start.1 = (bf16[512,2048]{1,0:T(8,128)(2,1)S(1)}, bf16[512,2048]{1,0:T(8,128)(2,1)}, u32[]{:S(2)}) copy-start(bf16[512,2048]{1,0:T(8,128)(2,1)} %param.10) | copy-start | bytes 6291460
  208.5 2.7 %copy-start.2 = (bf16[1,256,1024]{2,1,0:T(8,128)(2,1)S(1)}, bf16[1,256,1024]{2,1,0:T(8,128)(2,1)}, u32[]{:S(2)}) copy-start(bf16[1,256,1024]{2,1,0:T(8,128)(2,1)} %param.12) | copy-start | bytes 1572868
  208.5 2.7 %copy-start.3 = (bf16[1,256,1024]{2,1,0:T(8,128)(2,1)S(1)}, bf16[1,256,1024]{2,1,0:T(8,128)(2,1)}, u32[]{:S(2)}) copy-start(bf16[1,256,1024]{2,1,0:T(8,128)(2,1)} %param.11) | copy-start | bytes 1572868
  212.7 37.4 %all-to-all-start.2 = ((bf16[64,8,256]{2,1,0:T(8,128)(2,1)}), bf16[64,8,256]{2,1,0:T(8,128)(2,1)S(1)}, u32[]{:S(2)}, u32[]{:S(2)}) async-start(bf16[64,8,256]{2,1,0:T(8,128)(2,1)} %fusion.15), calls=%async_computation.2 | async-start | bytes 524288 | tf_op jit(solution)/shard_map/all_to_all | solution.py:54
Sparse Core Ops, SparseCore 0:
  70.1 138.4 all-reduce.1
where the time goes:
time: 259 us
  waiting for transfers between devices  173 us (67%)
  starting transfers between devices  51.8 us (20%)
  between operations  14.1 us (5%)
  local copies, waits for them, and re-layouts  8.74 us (3%)
  other arithmetic  6.29 us (2%)
  matrix products  5.1 us (2%)
    psum x1, waiting for transfers between devices, per_device(): hidden_grad = lax.psum(partial_grad, 'dp')  139 us
    all_to_all x1, starting transfers between devices, per_device(): lax.all_to_all(out_scales, 'expert', split_axis=0, concat_axis=0, tiled=T...  23.5 us
    all_to_all x1, starting transfers between devices, per_device(): lax.all_to_all(slot_grad, 'expert', split_axis=0, concat_axis=0, tiled=True)  23.5 us
    all_to_all x1, waiting for transfers between devices, per_device(): lax.all_to_all(out_values, 'expert', split_axis=0, concat_axis=0, tiled=T...  13.7 us
    all_to_all x1, waiting for transfers between devices, per_device(): lax.all_to_all(slot_grad, 'expert', split_axis=0, concat_axis=0, tiled=True)  11.3 us
    all_to_all x1, waiting for transfers between devices, per_device(): lax.all_to_all(out_scales, 'expert', split_axis=0, concat_axis=0, tiled=T...  9.1 us
  transfers between devices with their start and end apart: 4, of which 4 were waited for; matrix products, arithmetic and copies ran while one was open for 2% of the time, Pallas kernels for 0%

commit v1 on v0

v1 whole, which is shorter than its diff:
```python
import jax
import jax.numpy as jnp
from jax import lax
from jax.experimental import pallas as pl
from jax.experimental.pallas import tpu as pltpu
from jax.sharding import PartitionSpec as P

MESH = pl.DeviceIdType.MESH
F32, BF16 = jnp.float32, jnp.bfloat16

RING = 8
CAP = 8

REDUCE_RIGHT = ((0, 4), (1, 3), (0, 3), (1, 2), (0, 2), (1, 1), (0, 1))
REDUCE_LEFT = ((1, 4), (0, 3), (1, 3), (0, 2), (1, 2), (0, 1), (1, 1))
GATHER_RIGHT = ((0, 1), (1, 1), (0, 2), (1, 2), (0, 3), (1, 3), (0, 4))
GATHER_LEFT = ((1, 1), (0, 1), (1, 2), (0, 2), (1, 3), (0, 3), (1, 4))


def kernel(
    ids_ref,
    dy_ref,
    scale_ref,
    saved_hbm,
    gate_hbm,
    up_hbm,
    down_hbm,
    gi_out,
    gd_out,
    saved,
    w_gate,
    w_up,
    w_down,
    pick,
    send,
    recv,
    received,
    hidden,
    c_gate,
    c_up,
    part,
    rs_send,
    rs_recv,
    acc,
    z_send,
    z_recv,
    grads,
    back_send,
    back_recv,
    gd,
    gi,
    in_sem,
    out_sem,
    a2a_sem,
    rs_ssem,
    rs_rsem,
    z_sem,
    ag_ssem,
    ag_rsem,
    back_sem,
):
    experts = send.shape[0]
    slots, feats = received.shape
    ff = hidden.shape[1]
    half_ff = ff // 2
    chunk = slots // RING
    per_chunk = chunk // CAP
    rows = dy_ref.shape[0]

    me = lax.axis_index("expert")
    dp = lax.axis_index("dp")
    x = lax.rem(dp, RING)
    base = dp - x
    right = base + lax.rem(x + 1, RING)
    left = base + lax.rem(x + RING - 1, RING)
    other = lax.rem(dp + RING, 2 * RING)

    loads = [
        pltpu.make_async_copy(src, dst, in_sem.at[k])
        for k, (src, dst) in enumerate(
            ((saved_hbm, saved), (down_hbm, w_down), (gate_hbm, w_gate), (up_hbm, w_up))
        )
    ]
    for load in loads:
        load.start()

    barrier = pltpu.get_barrier_semaphore()

    def greet(i, carry):
        pl.semaphore_signal(
            barrier, inc=1, device_id={"expert": lax.rem(me + i, experts)}, device_id_type=MESH
        )
        return carry

    lax.fori_loop(1, experts, greet, 0)
    for peer in (right, left, other):
        pl.semaphore_signal(barrier, inc=1, device_id={"dp": peer}, device_id_type=MESH)

    ids = ids_ref[...]
    named = jnp.where(lax.broadcasted_iota(jnp.int32, (experts, rows), 0) == ids, 1.0, 0.0)
    before = jnp.where(
        lax.broadcasted_iota(jnp.int32, (rows, rows), 0)
        < lax.broadcasted_iota(jnp.int32, (rows, rows), 1),
        1.0,
        0.0,
    ).astype(BF16)
    earlier = jnp.dot(named.astype(BF16), before, preferred_element_type=F32)
    rank = jnp.sum(earlier * named, axis=0, keepdims=True)
    position = ids * CAP + rank.astype(jnp.int32)
    hit = lax.broadcasted_iota(jnp.int32, (slots, rows), 0) == position
    pick[...] = jnp.where(hit, 1.0, 0.0).astype(BF16)
    halves = []
    for h in range(2):
        scaled = jnp.where(hit, scale_ref[h : h + 1, :].astype(F32), 0.0).astype(BF16)
        rows_h = jnp.dot(
            scaled, dy_ref[:, h * 128 : (h + 1) * 128], preferred_element_type=F32
        )
        halves.append(rows_h.reshape(experts, CAP, 128))
    send[...] = jnp.concatenate(halves, axis=1).astype(BF16)

    pl.semaphore_wait(barrier, experts - 1 + 3)

    def dispatch(i, carry):
        to = lax.rem(me + i, experts)
        pltpu.make_async_remote_copy(
            src_ref=send.at[to],
            dst_ref=recv.at[me],
            send_sem=a2a_sem.at[0],
            recv_sem=a2a_sem.at[1],
            device_id={"expert": to},
            device_id_type=MESH,
        ).start()
        return carry

    lax.fori_loop(1, experts, dispatch, 0)
    recv[pl.ds(me, 1)] = send[pl.ds(me, 1)]

    loads[0].wait()
    step = 16

    def activate(i, carry):
        at = pl.ds(pl.multiple_of(i * step, step), step)
        gate = saved[at, :ff].astype(F32)
        up = saved[at, ff:].astype(F32)
        sig = jax.nn.sigmoid(gate)
        silu = gate * sig
        c_up[at, :] = silu
        c_gate[at, :] = up * sig * (1.0 + gate * (1.0 - sig))
        hidden[at, :] = (silu * up).astype(BF16)
        return carry

    lax.fori_loop(0, slots // step, activate, 0)

    def all_but_one(buf_a, buf_b, sems):
        n = pl.ds(0, experts - 1)
        return pltpu.make_async_remote_copy(
            src_ref=buf_a.at[n],
            dst_ref=buf_b.at[n],
            send_sem=sems.at[0],
            recv_sem=sems.at[1],
            device_id={"expert": lax.rem(me + 1, experts)},
            device_id_type=MESH,
        )

    arrived = all_but_one(send, recv, a2a_sem)
    arrived.wait_recv()
    got = recv[...].astype(F32)
    received[...] = jnp.concatenate(
        [got[:, :CAP].reshape(slots, 128), got[:, CAP:].reshape(slots, 128)], axis=1
    ).astype(BF16)

    loads[1].wait()
    block = 128

    def project(i, carry):
        at = pl.ds(pl.multiple_of(i * block, block), block)
        part[at, :] = jnp.dot(received[at, :], w_down[...], preferred_element_type=F32)
        return carry

    lax.fori_loop(0, slots // block, project, 0)

    def own(c, h):
        at = pl.ds(pl.multiple_of(c * chunk, chunk), chunk)
        return part[at, h * half_ff : (h + 1) * half_ff]

    sides = ((right, REDUCE_RIGHT, 1), (left, REDUCE_LEFT, RING - 1))

    def rs_copy(side, k):
        return pltpu.make_async_remote_copy(
            src_ref=rs_send.at[side, k],
            dst_ref=rs_recv.at[side, k],
            send_sem=rs_ssem.at[side, k],
            recv_sem=rs_rsem.at[side, k],
            device_id={"dp": sides[side][0]},
            device_id_type=MESH,
        )

    for k in range(7):
        for side in range(2):
            h, hops = sides[side][1][k]
            c = lax.rem(x + hops * sides[side][2], RING)
            value = own(c, h)
            if k >= 2:
                rs_copy(side, k - 2).wait_recv()
                value = value + rs_recv[side, k - 2].astype(F32)
            rs_send[side, k] = value.astype(BF16)
            rs_copy(side, k).start()
        if k == 1:

            def weight_grad(i, carry):
                at = pl.ds(pl.multiple_of(i * 256, 256), 256)
                gd[:, at] = lax.dot_general(
                    received[...],
                    hidden[:, at],
                    (((0,), (0,)), ((), ())),
                    preferred_element_type=F32,
                )
                return carry

            lax.fori_loop(0, ff // 256, weight_grad, 0)
            gd_copy = pltpu.make_async_copy(gd, gd_out, out_sem.at[0])
            gd_copy.start()

    def z_copy(h):
        return pltpu.make_async_remote_copy(
            src_ref=z_send.at[h],
            dst_ref=z_recv.at[h],
            send_sem=z_sem.at[0, h],
            recv_sem=z_sem.at[1, h],
            device_id={"dp": other},
            device_id_type=MESH,
        )

    for h in (1, 0):
        total = own(x, h)
        for side in range(2):
            k = sides[side][1].index((h, 1))
            rs_copy(side, k).wait_recv()
            total = total + rs_recv[side, k].astype(F32)
        acc[h] = total
        z_send[h] = total.astype(BF16)
        z_copy(h).start()

    ways = ((right, GATHER_RIGHT, RING - 1), (left, GATHER_LEFT, 1))

    def ag_copy(side, h, hops):
        k = ways[side][1].index((h, hops))
        c = lax.rem(x + (hops - 1) * ways[side][2], RING)
        return pltpu.make_async_remote_copy(
            src_ref=grads.at[c, h],
            dst_ref=grads.at[c, h],
            send_sem=ag_ssem.at[side, k],
            recv_sem=ag_rsem.at[side, k],
            device_id={"dp": ways[side][0]},
            device_id_type=MESH,
        )

    for h in (1, 0):
        z_copy(h).wait_recv()
        grads[x, h] = (acc[h] + z_recv[h].astype(F32)).astype(BF16)
        for side in range(2):
            ag_copy(side, h, 1).start()

    loads[2].wait()
    loads[3].wait()

    def finish(chunks):
        d_gate, d_up = [], []
        for c in chunks:
            at = pl.ds(pl.multiple_of(c * chunk, chunk), chunk)
            g = jnp.concatenate([grads[c, 0], grads[c, 1]], axis=1).astype(F32)
            d_gate.append((g * c_gate[at, :]).astype(BF16))
            d_up.append((g * c_up[at, :]).astype(BF16))
        if len(chunks) > 1:
            d_gate, d_up = [jnp.concatenate(d_gate, axis=0)], [jnp.concatenate(d_up, axis=0)]
        across = (((1,), (1,)), ((), ()))
        out = lax.dot_general(d_gate[0], w_gate[...], across, preferred_element_type=F32)
        out = out + lax.dot_general(d_up[0], w_up[...], across, preferred_element_type=F32)
        for n, c in enumerate(chunks):
            mine = out[n * chunk : (n + 1) * chunk]
            first = c * per_chunk
            back_send[pl.ds(first, per_chunk)] = jnp.concatenate(
                [
                    mine[:, :128].reshape(per_chunk, CAP, 128),
                    mine[:, 128:].reshape(per_chunk, CAP, 128),
                ],
                axis=1,
            ).astype(BF16)

            def give_back(i, carry):
                to = first + i

                @pl.when(to != me)
                def _():
                    pltpu.make_async_remote_copy(
                        src_ref=back_send.at[to],
                        dst_ref=back_recv.at[me],
                        send_sem=back_sem.at[0],
                        recv_sem=back_sem.at[1],
                        device_id={"expert": to},
                        device_id_type=MESH,
                    ).start()

                return carry

            lax.fori_loop(0, per_chunk, give_back, 0)

    finish([x])
    for hops in range(1, RING // 2 + 1):
        for n in range(2):
            for side in range(2):
                h = n if side == 0 else 1 - n
                if (h, hops) in ways[side][1]:
                    ag_copy(side, h, hops).wait_recv()
                    if (h, hops + 1) in ways[side][1]:
                        ag_copy(side, h, hops + 1).start()
        if hops < RING // 2:
            finish([lax.rem(x + RING - hops, RING), lax.rem(x + hops, RING)])
        else:
            finish([lax.rem(x + hops, RING)])

    back_recv[pl.ds(me, 1)] = back_send[pl.ds(me, 1)]
    returned = all_but_one(back_send, back_recv, back_sem)
    returned.wait_recv()
    got = back_recv[...].astype(F32)
    table = jnp.concatenate(
        [got[:, :CAP].reshape(slots, 128), got[:, CAP:].reshape(slots, 128)], axis=1
    ).astype(BF16)
    gi[...] = lax.dot_general(
        pick[...], table, (((0,), (0,)), ((), ())), preferred_element_type=F32
    ).astype(BF16)
    gi_copy = pltpu.make_async_copy(gi, gi_out, out_sem.at[1])
    gi_copy.start()

    arrived.wait_send()
    returned.wait_send()
    for side in range(2):
        for k in range(7):
            rs_copy(side, k).wait_send()
        for h, hops in ways[side][1]:
            ag_copy(side, h, hops).wait_send()
    for h in range(2):
        z_copy(h).wait_send()
    gd_copy.wait()
    gi_copy.wait()


def per_device(dy_values, dy_scales, expert_ids, saved_pre, w_gate, w_up, w_down):
    rows, feats = dy_values.shape
    slots = saved_pre.shape[0]
    ff = w_down.shape[2]
    experts = slots // CAP
    chunk = slots // RING
    vmem = pl.BlockSpec(memory_space=pltpu.VMEM)
    anywhere = pl.BlockSpec(memory_space=pl.ANY)
    grad_input, grad_down = pl.pallas_call(
        kernel,
        out_shape=(
            jax.ShapeDtypeStruct((rows, feats), BF16),
            jax.ShapeDtypeStruct((feats, ff), F32),
        ),
        in_specs=[vmem] * 3 + [anywhere] * 4,
        out_specs=(anywhere, anywhere),
        scratch_shapes=[
            pltpu.VMEM((slots, 2 * ff), BF16),
            pltpu.VMEM((feats, ff), BF16),
            pltpu.VMEM((feats, ff), BF16),
            pltpu.VMEM((feats, ff), BF16),
            pltpu.VMEM((slots, rows), BF16),
            pltpu.VMEM((experts, 2 * CAP, 128), BF16),
            pltpu.VMEM((experts, 2 * CAP, 128), BF16),
            pltpu.VMEM((slots, feats), BF16),
            pltpu.VMEM((slots, ff), BF16),
            pltpu.VMEM((slots, ff), F32),
            pltpu.VMEM((slots, ff), F32),
            pltpu.VMEM((slots, ff), F32),
            pltpu.VMEM((2, 7, chunk, ff // 2), BF16),
            pltpu.VMEM((2, 7, chunk, ff // 2), BF16),
            pltpu.VMEM((2, chunk, ff // 2), F32),
            pltpu.VMEM((2, chunk, ff // 2), BF16),
            pltpu.VMEM((2, chunk, ff // 2), BF16),
            pltpu.VMEM((RING, 2, chunk, ff // 2), BF16),
            pltpu.VMEM((experts, 2 * CAP, 128), BF16),
            pltpu.VMEM((experts, 2 * CAP, 128), BF16),
            pltpu.VMEM((feats, ff), F32),
            pltpu.VMEM((rows, feats), BF16),
            pltpu.SemaphoreType.DMA((4,)),
            pltpu.SemaphoreType.DMA((2,)),
            pltpu.SemaphoreType.DMA((2,)),
            pltpu.SemaphoreType.DMA((2, 7)),
            pltpu.SemaphoreType.DMA((2, 7)),
            pltpu.SemaphoreType.DMA((2, 2)),
            pltpu.SemaphoreType.DMA((2, 7)),
            pltpu.SemaphoreType.DMA((2, 7)),
            pltpu.SemaphoreType.DMA((2,)),
        ],
        compiler_params=pltpu.CompilerParams(
            collective_id=0, has_side_effects=True, vmem_limit_bytes=60 * 1024 * 1024
        ),
        name="experts_backward",
    )(
        expert_ids.reshape(1, rows),
        dy_values,
        dy_scales.T,
        saved_pre,
        w_gate[0],
        w_up[0],
        w_down[0],
    )
    return grad_input, grad_down[None]


def solution(mesh):
    return jax.shard_map(
        per_device,
        mesh=mesh,
        in_specs=(
            P("expert", "dp"),
            P("expert", "dp"),
            P("expert", None),
            P("expert", None),
            P("expert", "dp", None),
            P("expert", "dp", None),
            P("expert", "dp", None),
        ),
        out_specs=(P("expert", "dp"), P("expert", "dp", None)),
        check_vma=False,
    )
```

time: 259 us -> 83.7 us (0.32)
  the two profiles are of different devices: /device:TPU:1 before, /device:TPU:9 now
where the time goes in v1:
time: 83.7 us; the launch traced here: 83.5 us
  Pallas kernels  79 us (94%)
  local copies, waits for them, and re-layouts  3.87 us (5%)
    pallas_call x1, Pallas kernels, per_device(): pl.pallas_call(kernel, out_shape=(jax.ShapeDtypeStruct((rows, feats), BF1...  79 us
    unnamed x2, local copies, waits for them, and re-layouts  3.87 us

profile of v1, /device:TPU:9, one launch (start us, length us, event | category | flops | bytes accessed | tf_op | source)
XLA Modules:
  0.0 83.5 jit_solution(5279610028497521604)
XLA Ops:
  0.6 79.0 %experts_backward.1 = (bf16[256,256]{1,0:T(8,128)(2,1)}, f32[256,1024]{1,0:T(8,128)}) custom-call(s32[1,256]{1,0:T(1,128)} %bitcast.10, bf16[256,256]{1,0:T(8,128)(2,1)} %dy_ref.1, bf16[2,256]{1,0:T(2,128)(2,1)} %bitcast.11, bf16[512,2048]{1,0:T(8,128)(2,1)} %saved_hbm.1, bf16[256,1024]{1,0:T(8,128)(2,1)} %bitcast.7, bf16[256,1024]{1,0:T(8,128)(2,1)} %bitcast.8, ...), custom_call_target="tpu_custom_call" | custom-call | tf_op jit(solution)/shard_map/experts_backward/pallas_call | solution.py:356
  79.6 1.6 %copy.11 = bf16[256,256]{1,0:T(8,128)(2,1)} copy(bf16[256,256]{1,0:T(8,128)(2,1)} %get-tuple-element.8) | data formatting | bytes 262144
  81.2 2.3 %copy.12 = f32[1,256,1024]{2,1,0:T(8,128)} copy(f32[1,256,1024]{2,1,0:T(8,128)} %bitcast.6) | data formatting | bytes 2097152

commit v2 on v1

--- a/solution.py
+++ b/solution.py
@@ -25,8 +25,8 @@
     gate_hbm,
     up_hbm,
     down_hbm,
-    gi_out,
-    gd_out,
+    gi,
+    gd,
     saved,
     w_gate,
     w_up,
@@ -47,10 +47,7 @@
     grads,
     back_send,
     back_recv,
-    gd,
-    gi,
     in_sem,
-    out_sem,
     a2a_sem,
     rs_ssem,
     rs_rsem,
@@ -218,8 +215,6 @@
                 return carry
 
             lax.fori_loop(0, ff // 256, weight_grad, 0)
-            gd_copy = pltpu.make_async_copy(gd, gd_out, out_sem.at[0])
-            gd_copy.start()
 
     def z_copy(h):
         return pltpu.make_async_remote_copy(
@@ -329,8 +324,6 @@
     gi[...] = lax.dot_general(
         pick[...], table, (((0,), (0,)), ((), ())), preferred_element_type=F32
     ).astype(BF16)
-    gi_copy = pltpu.make_async_copy(gi, gi_out, out_sem.at[1])
-    gi_copy.start()
 
     arrived.wait_send()
     returned.wait_send()
@@ -341,8 +334,19 @@
             ag_copy(side, h, hops).wait_send()
     for h in range(2):
         z_copy(h).wait_send()
-    gd_copy.wait()
-    gi_copy.wait()
+
+
+def hand_over(gi_in, gd_in, gi_out, gd_out, sem):
+    cuts = sem.shape[0] - 1
+    tall = gd_in.shape[0] // cuts
+    copies = [pltpu.make_async_copy(gi_in, gi_out, sem.at[cuts])]
+    for k in range(cuts):
+        at = pl.ds(k * tall, tall)
+        copies.append(pltpu.make_async_copy(gd_in.at[at], gd_out.at[at], sem.at[k]))
+    for copy in copies:
+        copy.start()
+    for copy in copies:
+        copy.wait()
 
 
 def per_device(dy_values, dy_scales, expert_ids, saved_pre, w_gate, w_up, w_down):
@@ -353,14 +357,15 @@
     chunk = slots // RING
     vmem = pl.BlockSpec(memory_space=pltpu.VMEM)
     anywhere = pl.BlockSpec(memory_space=pl.ANY)
-    grad_input, grad_down = pl.pallas_call(
+    shapes = (
+        jax.ShapeDtypeStruct((rows, feats), BF16),
+        jax.ShapeDtypeStruct((feats, ff), F32),
+    )
+    results = pl.pallas_call(
         kernel,
-        out_shape=(
-            jax.ShapeDtypeStruct((rows, feats), BF16),
-            jax.ShapeDtypeStruct((feats, ff), F32),
-        ),
+        out_shape=tuple(pltpu.VMEM(shape.shape, shape.dtype) for shape in shapes),
         in_specs=[vmem] * 3 + [anywhere] * 4,
-        out_specs=(anywhere, anywhere),
+        out_specs=(vmem, vmem),
         scratch_shapes=[
             pltpu.VMEM((slots, 2 * ff), BF16),
             pltpu.VMEM((feats, ff), BF16),
@@ -382,10 +387,7 @@
             pltpu.VMEM((RING, 2, chunk, ff // 2), BF16),
             pltpu.VMEM((experts, 2 * CAP, 128), BF16),
             pltpu.VMEM((experts, 2 * CAP, 128), BF16),
-            pltpu.VMEM((feats, ff), F32),
-            pltpu.VMEM((rows, feats), BF16),
             pltpu.SemaphoreType.DMA((4,)),
-            pltpu.SemaphoreType.DMA((2,)),
             pltpu.SemaphoreType.DMA((2,)),
             pltpu.SemaphoreType.DMA((2, 7)),
             pltpu.SemaphoreType.DMA((2, 7)),
@@ -407,6 +409,15 @@
         w_up[0],
         w_down[0],
     )
+    grad_input, grad_down = pl.pallas_call(
+        hand_over,
+        out_shape=shapes,
+        in_specs=[vmem, vmem],
+        out_specs=(anywhere, anywhere),
+        scratch_shapes=[pltpu.SemaphoreType.DMA((5,))],
+        compiler_params=pltpu.CompilerParams(vmem_limit_bytes=4 * 1024 * 1024),
+        name="hand_over",
+    )(*results)
     return grad_input, grad_down[None]
 
 

time: 83.7 us -> 80.2 us (0.958)
  local copies, waits for them, and re-layouts: 3.87 us -> 0 us
    unnamed x2 -> x0, local copies, waits for them, and re-layouts: 3.87 us -> none
    pallas_call x1 -> x2, Pallas kernels: 79 us -> 79.4 us  [the longest x1 78.4 us: per_device(): pl.pallas_call(kernel, out_shape=tuple((pltpu.VMEM(shape.shape, shape.dty...]
where the time goes in v2:
time: 80.2 us; the launch traced here: 80 us
  Pallas kernels  79.4 us (99%)
    pallas_call x1, Pallas kernels, per_device(): pl.pallas_call(kernel, out_shape=tuple((pltpu.VMEM(shape.shape, shape.dty...  78.4 us

profile of v2, /device:TPU:9, one launch (start us, length us, event | category | flops | bytes accessed | tf_op | source)
XLA Modules:
  0.0 80.0 jit_solution(3596033379449694714)
XLA Ops:
  0.6 78.4 %experts_backward.1 = (bf16[256,256]{1,0:T(8,128)(2,1)S(1)}, f32[256,1024]{1,0:T(8,128)S(1)}) custom-call(s32[1,256]{1,0:T(1,128)} %bitcast.9, bf16[256,256]{1,0:T(8,128)(2,1)} %dy_ref.1, bf16[2,256]{1,0:T(2,128)(2,1)} %bitcast.10, bf16[512,2048]{1,0:T(8,128)(2,1)} %saved_hbm.1, bf16[256,1024]{1,0:T(8,128)(2,1)} %bitcast.6, bf16[256,1024]{1,0:T(8,128)(2,1)} %bitcast.7, ...), custom_call_target="tpu_custom_call" | custom-call | tf_op jit(solution)/shard_map/experts_backward/pallas_call | solution.py:364
  79.0 1.0 %hand_over.1 = (bf16[256,256]{1,0:T(8,128)(2,1)}, f32[256,1024]{1,0:T(8,128)}) custom-call(bf16[256,256]{1,0:T(8,128)(2,1)S(1)} %get-tuple-element.6.gi_in, f32[256,1024]{1,0:T(8,128)S(1)} %get-tuple-element.7.gd_in), custom_call_target="tpu_custom_call" | custom-call | tf_op jit(solution)/shard_map/hand_over/pallas_call | solution.py:412

commit v3 on v2

--- a/solution.py
+++ b/solution.py
@@ -10,6 +10,7 @@
 
 RING = 8
 CAP = 8
+Z_HI, Y, CORES = 4, 8, 2
 
 REDUCE_RIGHT = ((0, 4), (1, 3), (0, 3), (1, 2), (0, 2), (1, 1), (0, 1))
 REDUCE_LEFT = ((1, 4), (0, 3), (1, 3), (0, 2), (1, 2), (0, 1), (1, 1))
@@ -83,13 +84,21 @@
 
     barrier = pltpu.get_barrier_semaphore()
 
+    def centred(k, size):
+        step = (k + 1) // 2
+        return size // 2 + step - 2 * step * lax.rem(k, 2)
+
+    def nth(k):
+        core = lax.rem(me + 1 + k, CORES)
+        y = lax.rem(me // CORES + centred(k // CORES % Y, Y), Y)
+        z = lax.rem(me // (CORES * Y) + centred(k // (CORES * Y), Z_HI), Z_HI)
+        return (z * Y + y) * CORES + core
+
     def greet(i, carry):
-        pl.semaphore_signal(
-            barrier, inc=1, device_id={"expert": lax.rem(me + i, experts)}, device_id_type=MESH
-        )
+        pl.semaphore_signal(barrier, inc=1, device_id={"expert": nth(i)}, device_id_type=MESH)
         return carry
 
-    lax.fori_loop(1, experts, greet, 0)
+    lax.fori_loop(0, experts - 1, greet, 0)
     for peer in (right, left, other):
         pl.semaphore_signal(barrier, inc=1, device_id={"dp": peer}, device_id_type=MESH)
 
@@ -118,7 +127,7 @@
     pl.semaphore_wait(barrier, experts - 1 + 3)
 
     def dispatch(i, carry):
-        to = lax.rem(me + i, experts)
+        to = nth(i)
         pltpu.make_async_remote_copy(
             src_ref=send.at[to],
             dst_ref=recv.at[me],
@@ -129,7 +138,7 @@
         ).start()
         return carry
 
-    lax.fori_loop(1, experts, dispatch, 0)
+    lax.fori_loop(0, experts - 1, dispatch, 0)
     recv[pl.ds(me, 1)] = send[pl.ds(me, 1)]
 
     loads[0].wait()

time: 80.2 us -> 78.2 us (0.975)
  Pallas kernels: 79.4 us -> 77.4 us
    pallas_call x1, Pallas kernels: 78.4 us -> 76.3 us  [per_device(): pl.pallas_call(kernel, out_shape=tuple((pltpu.VMEM(shape.shape, shape.dty...]
where the time goes in v3:
time: 78.2 us; the launch traced here: 78 us
  Pallas kernels  77.4 us (99%)
    pallas_call x1, Pallas kernels, per_device(): pl.pallas_call(kernel, out_shape=tuple((pltpu.VMEM(shape.shape, shape.dty...  76.3 us

profile of v3, /device:TPU:9, one launch (start us, length us, event | category | flops | bytes accessed | tf_op | source)
XLA Modules:
  0.0 78.0 jit_solution(17269436999737166670)
XLA Ops:
  0.6 76.3 %experts_backward.1 = (bf16[256,256]{1,0:T(8,128)(2,1)S(1)}, f32[256,1024]{1,0:T(8,128)S(1)}) custom-call(s32[1,256]{1,0:T(1,128)} %bitcast.9, bf16[256,256]{1,0:T(8,128)(2,1)} %dy_ref.1, bf16[2,256]{1,0:T(2,128)(2,1)} %bitcast.10, bf16[512,2048]{1,0:T(8,128)(2,1)} %saved_hbm.1, bf16[256,1024]{1,0:T(8,128)(2,1)} %bitcast.6, bf16[256,1024]{1,0:T(8,128)(2,1)} %bitcast.7, ...), custom_call_target="tpu_custom_call" | custom-call | tf_op jit(solution)/shard_map/experts_backward/pallas_call | solution.py:373
  77.0 1.0 %hand_over.1 = (bf16[256,256]{1,0:T(8,128)(2,1)}, f32[256,1024]{1,0:T(8,128)}) custom-call(bf16[256,256]{1,0:T(8,128)(2,1)S(1)} %get-tuple-element.6.gi_in, f32[256,1024]{1,0:T(8,128)S(1)} %get-tuple-element.7.gd_in), custom_call_target="tpu_custom_call" | custom-call | tf_op jit(solution)/shard_map/hand_over/pallas_call | solution.py:421

commit v4 on v3

--- a/solution.py
+++ b/solution.py
@@ -86,7 +86,7 @@
 
     def centred(k, size):
         step = (k + 1) // 2
-        return size // 2 + step - 2 * step * lax.rem(k, 2)
+        return size // 2 + (step - 2 * step * lax.rem(k, 2)) * (1 - 2 * lax.rem(me, CORES))
 
     def nth(k):
         core = lax.rem(me + 1 + k, CORES)

time: 78.2 us -> 78 us (level)
  no operation moved by 1% of the time
where the time goes in v4:
time: 78 us; the launch traced here: 77.9 us
  Pallas kernels  77.2 us (99%)
    pallas_call x1, Pallas kernels, per_device(): pl.pallas_call(kernel, out_shape=tuple((pltpu.VMEM(shape.shape, shape.dty...  76.2 us

profile of v4, /device:TPU:9, one launch (start us, length us, event | category | flops | bytes accessed | tf_op | source)
XLA Modules:
  0.0 77.9 jit_solution(1542766285571222663)
XLA Ops:
  0.6 76.2 %experts_backward.1 = (bf16[256,256]{1,0:T(8,128)(2,1)S(1)}, f32[256,1024]{1,0:T(8,128)S(1)}) custom-call(s32[1,256]{1,0:T(1,128)} %bitcast.9, bf16[256,256]{1,0:T(8,128)(2,1)} %dy_ref.1, bf16[2,256]{1,0:T(2,128)(2,1)} %bitcast.10, bf16[512,2048]{1,0:T(8,128)(2,1)} %saved_hbm.1, bf16[256,1024]{1,0:T(8,128)(2,1)} %bitcast.6, bf16[256,1024]{1,0:T(8,128)(2,1)} %bitcast.7, ...), custom_call_target="tpu_custom_call" | custom-call | tf_op jit(solution)/shard_map/experts_backward/pallas_call | solution.py:373
  76.8 1.0 %hand_over.1 = (bf16[256,256]{1,0:T(8,128)(2,1)}, f32[256,1024]{1,0:T(8,128)}) custom-call(bf16[256,256]{1,0:T(8,128)(2,1)S(1)} %get-tuple-element.6.gi_in, f32[256,1024]{1,0:T(8,128)S(1)} %get-tuple-element.7.gd_in), custom_call_target="tpu_custom_call" | custom-call | tf_op jit(solution)/shard_map/hand_over/pallas_call | solution.py:421
